TPU v7x, 256 devices: a whole 4x4x8 slice. The times are simulated.
256 devices in a mesh: dp: 2 (over x_lo), ctx: 16 (over z, core), exp: 8 (over y, x_hi).
Axes of the slice: x: 4 (x_hi: 2, x_lo: 2; x = x_hi * 2 + x_lo), y: 4, z: 8, core: 2. Of those that a mesh axis runs over, the one named last changes fastest.
Arguments:
- queries: bfloat16 [512, 6144], P(('dp', 'ctx'), 'exp'), parts along dimension 0, may hold values from -150 to 150
- span_keys: bfloat16 [512, 1024], P(('dp', 'ctx'), 'exp'), parts along dimension 0, may hold values from -5 to 5
- span_values: bfloat16 [512, 1024], P(('dp', 'ctx'), 'exp'), parts along dimension 0, may hold values from -5 to 5
- cache_keys: bfloat16 [131072, 1024], P(('dp', 'ctx'), 'exp'), parts along dimension 0, may hold values from -5 to 5
- cache_values: bfloat16 [131072, 1024], P(('dp', 'ctx'), 'exp'), parts along dimension 0, may hold values from -5 to 5
- span_start: int32 [2], P('dp'), parts along dimension 0, may hold values from 16384 to 65536
- residual: bfloat16 [512, 6144], P(('dp', 'ctx', 'exp')), parts along dimension 0, may hold values from -40 to 40
- out_weight: bfloat16 [6144, 6144], P('exp', 'ctx'), may hold values from -0.078125 to 0.078125
- norm_gain: bfloat16 [6144], replicated, may hold values from 0.099609375 to 1.8984375
- router_weight: bfloat16 [6144, 4], replicated, may hold values from -0.078125 to 0.078125
- expert_ids: int32 [512, 2], P('dp'), parts along dimension 0, may hold values from 0 to 3, as said below
- gate_weight: bfloat16 [6144, 32768], P(None, ('ctx', 'exp')), may hold values from -0.078125 to 0.078125
- up_weight: bfloat16 [6144, 32768], P(None, ('ctx', 'exp')), may hold values from -0.078125 to 0.078125
- down_weight: bfloat16 [32768, 6144], P(('ctx', 'exp')), may hold values from -0.0625 to 0.0625
Outputs:
- mixed: bfloat16 [512, 6144], P(('dp', 'ctx', 'exp')), parts along dimension 0
There are 2 independent parts, one for each index of `dp`. A program takes and returns all parts, laid end to end along the dimension named above; an argument that names none is the same for every part. Nothing has to cross between parts.
Inputs may be any that keep to these rules, and one draw needn't show every extreme that they name: `expert_ids`: the two experts of a token differ.
All inputs are finite; a program needn't handle non-finite values.
Results may differ from a plain program's by a relative error of at most 0.013.
Values may be sent and summed in bfloat16 or wider, within the bound.
No kernel may reach another device: no remote copies, remote signals or barrier semaphores. Data moves between devices by JAX's collectives and lax.ppermute only.
A program may use at most 128 MiB of HBM per device.

v0:
```python
import math

import jax
import jax.numpy as jnp
from jax import lax
from jax.experimental import pallas as pl
from jax.experimental.pallas import tpu as pltpu
from jax.sharding import PartitionSpec as P

D = 6144
HEAD_DIM = 128
EXPERTS = 4
FF = 8192
TOPK = 2
SPAN = 256
CAP = 160
NZ = 8
NE = 8
FINE = 2
HEADS_LOCAL = 6
BLOCK_TOKENS = 16
BLOCK_ROWS = BLOCK_TOKENS * HEADS_LOCAL
ROWS = NZ * BLOCK_ROWS
Q_BLOCK = 256
CHUNK = 4096
NEAR = 256
FAR = 2.0**64
MESSAGE_ROWS = BLOCK_ROWS + 16
COLS = 768
HALF = 384
EPSILON = 1e-05
MASKED = -1e30
EXP2_SCALE = HEAD_DIM**-0.5 * math.log2(math.e)
BF16 = jnp.bfloat16
F32 = jnp.float32

Z_GROUPS = [[2 * z + core for z in range(NZ)] for core in range(2)]
SIBLINGS = [(c, c ^ 1) for c in range(2 * NZ)]


def exchange_z(blocks):
    return lax.all_to_all(blocks, "ctx", 0, 0, axis_index_groups=Z_GROUPS, tiled=True)


def exchange_exp(blocks):
    return lax.all_to_all(blocks, "exp", 0, 0, tiled=True)


def sibling(x):
    return lax.ppermute(x, "ctx", SIBLINGS)


VMEM = pl.BlockSpec(memory_space=pltpu.VMEM)
SMEM = pl.BlockSpec(memory_space=pltpu.SMEM)
ANY = pl.BlockSpec(memory_space=pl.ANY)


def in_hbm(x):
    return pltpu.with_memory_space_constraint(x, pltpu.HBM)


def in_vmem(x):
    return pltpu.with_memory_space_constraint(x, pltpu.VMEM)


def call(
    kernel,
    shape,
    *args,
    specs=None,
    space=jax.ShapeDtypeStruct,
    limit=32,
    flops=1 << 20,
    scratch=(),
):
    return pl.pallas_call(
        kernel,
        out_shape=space(shape, BF16),
        in_specs=specs or [VMEM] * len(args),
        out_specs=VMEM,
        scratch_shapes=scratch,
        compiler_params=pltpu.CompilerParams(vmem_limit_bytes=limit << 20),
        cost_estimate=pl.CostEstimate(flops=flops, bytes_accessed=1 << 20, transcendentals=0),
    )(*args)


def first_message_kernel(q, residual, out):
    res = residual[...].astype(F32)
    row = lax.broadcasted_iota(jnp.int32, (16, HEAD_DIM), 0)
    for z in range(NZ):
        for h in range(HEADS_LOCAL):
            out[z, h * BLOCK_TOKENS : (h + 1) * BLOCK_TOKENS, :] = q[
                :, h * HEAD_DIM : (h + 1) * HEAD_DIM
            ]
        rows = jnp.zeros((16, HEAD_DIM), F32)
        for j in range(COLS // HEAD_DIM):
            start = z * COLS + j * HEAD_DIM
            piece = res[:, start : start + HEAD_DIM]
            for f in range(FINE):
                rows = jnp.where(row == j * FINE + f, piece[f : f + 1, :], rows)
        out[z, BLOCK_ROWS:, :] = rows.astype(BF16)


def split3(x):
    first = x.astype(BF16).astype(F32)
    rest = x - first
    second = rest.astype(BF16).astype(F32)
    return first, second, rest - second


def prepare_kernel(v0, v1, k1, values, keys, sem):
    copy = pltpu.make_async_copy(k1, keys, sem)
    copy.start()
    for part, rows in enumerate((v0, v1)):
        values[part, :HEAD_DIM, :] = rows[...].T
        values[part, HEAD_DIM:, :] = jnp.ones((16, CHUNK), BF16)
    copy.wait()


def prepare(v0, v1, k1):
    return pl.pallas_call(
        prepare_kernel,
        out_shape=(
            pltpu.HBM((2, HEAD_DIM + 16, CHUNK), BF16),
            pltpu.HBM((CHUNK, HEAD_DIM), BF16),
        ),
        in_specs=[VMEM, VMEM, ANY],
        out_specs=(VMEM, ANY),
        scratch_shapes=[pltpu.SemaphoreType.DMA],
        compiler_params=pltpu.CompilerParams(vmem_limit_bytes=16 << 20),
        cost_estimate=pl.CostEstimate(flops=0, bytes_accessed=6 << 20, transcendentals=0),
    )(v0, v1, k1)


def attention_kernel(
    info, first, k0, k1, turned, sk, sv, out, q, keys, values, peak, carried, sems, again
):
    copies = []
    for part, source in enumerate((k0, k1)):
        copies.append(pltpu.make_async_copy(source, keys.at[part], sems.at[2 * part]))
        copies.append(
            pltpu.make_async_copy(turned.at[part], values.at[part], sems.at[2 * part + 1])
        )
    for copy in copies:
        copy.start()
    q[...] = first[:, :BLOCK_ROWS, :].reshape(ROWS, HEAD_DIM)
    blocks = ROWS // Q_BLOCK

    def columns(b):
        return slice(b * Q_BLOCK, (b + 1) * Q_BLOCK)

    def scores_of(rows, b):
        return lax.dot_general(
            rows, q[columns(b), :], (((1,), (1,)), ((), ())), preferred_element_type=F32
        )

    core = info[2]
    span_rows = 2 * BLOCK_TOKENS

    def begin():
        span_values = jnp.concatenate([sv[...].T, jnp.ones((16, span_rows), BF16)], axis=0)
        for b in range(blocks):
            row = lax.broadcasted_iota(jnp.int32, (span_rows, Q_BLOCK), 0)
            col = lax.broadcasted_iota(jnp.int32, (span_rows, Q_BLOCK), 1) + b * Q_BLOCK
            token = col // BLOCK_ROWS * span_rows + core * BLOCK_TOKENS + col % BLOCK_TOKENS
            allowed = info[3] + row <= token
            s = jnp.where(allowed, scores_of(sk[...], b), MASKED)
            top = jnp.max(s, axis=0, keepdims=True)
            w = jnp.where(allowed, jnp.exp2((s - top) * EXP2_SCALE), 0.0).astype(BF16)
            peak[:, columns(b)] = jnp.broadcast_to(top, (8, Q_BLOCK))
            carried[:, columns(b)] = jnp.dot(span_values, w, preferred_element_type=F32)

    def soften(s, b):
        before = peak[:1, columns(b)]
        top = jnp.maximum(before, jnp.max(s, axis=0, keepdims=True))
        peak[:, columns(b)] = jnp.broadcast_to(top, (8, Q_BLOCK))
        w = jnp.exp2((s - top) * EXP2_SCALE).astype(BF16)
        return w, jnp.exp2((before - top) * EXP2_SCALE)

    def soften_near(s, b, part):
        before = top = peak[:1, columns(b)]
        factor = None
        if part == 0:
            top = jnp.maximum(before, jnp.max(s[:NEAR], axis=0, keepdims=True))
            peak[:, columns(b)] = jnp.broadcast_to(top, (8, Q_BLOCK))
            factor = jnp.exp2((before - top) * EXP2_SCALE)
        return jnp.exp2((s - top) * EXP2_SCALE).astype(BF16), factor

    def run(parts, count, valid=None, near=False, wait=lambda i: None):
        items = [(part, b) for part in parts for b in range(blocks)]

        def scores(item):
            s = scores_of(keys[item[0], :count, :], item[1])
            if valid is not None:
                row = lax.broadcasted_iota(jnp.int32, (count, Q_BLOCK), 0)
                s = jnp.where(row < valid, s, MASKED)
            return s

        def gather(item, w, factor):
            part, b = item
            sums = jnp.dot(values[part, :, :count], w, preferred_element_type=F32)
            held = carried[:, columns(b)]
            carried[:, columns(b)] = (held if factor is None else held * factor) + sums

        wait(0)
        s = scores(items[0])
        wait(1)
        earlier = None
        for i, item in enumerate(items):
            later = scores(items[i + 1]) if i + 1 < len(items) else None
            current = soften_near(s, item[1], item[0]) if near else soften(s, item[1])
            if earlier is not None:
                gather(items[i - 1], *earlier)
            earlier, s = current, later
        gather(items[-1], *earlier)

    def wait_for(stage):
        for copy in copies[:1] if stage == 0 else copies[1:]:
            copy.wait()

    begin()
    everything = (info[0] == CHUNK) & (info[1] == CHUNK)
    again[0] = jnp.int32(1)

    @pl.when(everything)
    def _():
        run((0, 1), CHUNK, near=True, wait=wait_for)
        mass = carried[HEAD_DIM : HEAD_DIM + 1, :]
        far = jnp.max(jnp.where(mass < FAR, 0.0, 1.0))
        again[0] = (far > 0.5).astype(jnp.int32)

        @pl.when(again[0] == 1)
        def _():
            begin()

    @pl.when(jnp.logical_not(everything))
    def _():
        wait_for(0)
        wait_for(1)

    @pl.when(again[0] == 1)
    def _():
        @pl.loop(0, 2)
        def _(part):
            valid = info[part]

            @pl.when(valid == CHUNK)
            def _():
                run((part,), CHUNK)

            @pl.when((valid < CHUNK) & (valid > CHUNK // 2))
            def _():
                run((part,), CHUNK, valid)

            @pl.when((valid <= CHUNK // 2) & (valid > 0))
            def _():
                run((part,), CHUNK // 2, valid)

    rows = carried[:HEAD_DIM, :].T.astype(BF16)
    out[:, :BLOCK_ROWS, :] = rows.reshape(NZ, BLOCK_ROWS, HEAD_DIM)
    terms = split3(peak[:1, :]) + split3(carried[HEAD_DIM : HEAD_DIM + 1, :])
    row = lax.broadcasted_iota(jnp.int32, (16, ROWS), 0)
    stats = jnp.zeros((16, ROWS), F32)
    for i, term in enumerate(terms):
        stats = jnp.where(row == i, term, stats)
    for z in range(NZ):
        shifted = stats if z == 0 else pltpu.roll(stats, ROWS - z * BLOCK_ROWS, 1)
        out[z, BLOCK_ROWS:, :] = shifted[:, :HEAD_DIM].astype(BF16)


def combine_kernel(message, *refs):
    out = refs[len(refs) // 2]
    peaks, masses = [], []
    for z in range(NZ):
        r = message[z, BLOCK_ROWS:, :].astype(F32)
        peaks.append(r[0:1] + r[1:2] + r[2:3])
        masses.append(r[3:4] + r[4:5] + r[5:6])
    top = peaks[0]
    for z in range(1, NZ):
        top = jnp.maximum(top, peaks[z])
    factors = [jnp.exp2((p - top) * EXP2_SCALE) for p in peaks]
    total = factors[0] * masses[0]
    for z in range(1, NZ):
        total = total + factors[z] * masses[z]
    row = lax.broadcasted_iota(jnp.int32, (HEAD_DIM, HEAD_DIM), 0)
    shares = jnp.zeros((HEAD_DIM, HEAD_DIM), F32)
    for z in range(NZ):
        shares = jnp.where(row == z, factors[z] / total, shares)
    shares = shares.T
    rows = jnp.zeros((BLOCK_ROWS, HEAD_DIM), F32)
    for z in range(NZ):
        rows = rows + message[z, :BLOCK_ROWS, :].astype(F32) * shares[:BLOCK_ROWS, z : z + 1]
    rows = rows.astype(BF16)
    for h in range(HEADS_LOCAL):
        piece = rows[h * BLOCK_TOKENS : (h + 1) * BLOCK_TOKENS]
        for z in range(NZ):
            out[z, :, h * HEAD_DIM : (h + 1) * HEAD_DIM] = piece


def call_and_pass(kernel, shape, args, carried):
    count, first = len(carried), len(args)
    return pl.pallas_call(
        kernel,
        out_shape=[jax.ShapeDtypeStruct(shape, BF16)]
        + [jax.ShapeDtypeStruct(c.shape, c.dtype) for c in carried],
        in_specs=[VMEM] * first + [ANY] * count,
        out_specs=[VMEM] + [ANY] * count,
        input_output_aliases={first + i: 1 + i for i in range(count)},
        compiler_params=pltpu.CompilerParams(vmem_limit_bytes=16 << 20),
        cost_estimate=pl.CostEstimate(flops=1 << 20, bytes_accessed=1 << 20, transcendentals=0),
    )(*args, *carried)


def project_kernel(info, x, own, other, out):
    r = lax.broadcasted_iota(jnp.int32, (128, 128), 0)
    c = lax.broadcasted_iota(jnp.int32, (128, 128), 1)
    wanted = r % 16 // FINE * 16 + r // 16 * FINE + r % FINE
    turn = jnp.where(c == wanted, 1.0, 0.0).astype(BF16)
    rows = jnp.dot(turn, x[...].reshape(128, COLS), preferred_element_type=F32).astype(BF16)
    core = info[2]
    for weight, side in ((own, core), (other, 1 - core)):
        part = jnp.dot(rows, weight[...], preferred_element_type=F32).astype(BF16)
        out[:, :, pl.ds(pl.multiple_of(side * HALF, HALF), HALF)] = part.reshape(NE, 16, HALF)


def mid_kernel(parts, message, out):
    total = parts[0].astype(F32)
    for e in range(1, NE):
        total = total + parts[e].astype(F32)
    rows = message[:, BLOCK_ROWS:, :].reshape(128, HEAD_DIM)
    r = lax.broadcasted_iota(jnp.int32, (16, 128), 0)
    c = lax.broadcasted_iota(jnp.int32, (16, 128), 1)
    for j in range(COLS // HEAD_DIM):
        pick = jnp.where(c == r // FINE * 16 + j * FINE + r % FINE, 1.0, 0.0).astype(BF16)
        place = slice(j * HEAD_DIM, (j + 1) * HEAD_DIM)
        res = jnp.dot(pick, rows, preferred_element_type=F32)
        mid = (res + total[:, place]).astype(BF16)
        for z in range(NZ):
            out[z, :, place] = mid


def norm_kernel(info, parts, gain, *refs):
    out, own = refs[len(refs) // 2 - 1 : len(refs) // 2 + 1]
    squares = jnp.zeros((16, 1), F32)
    for z in range(NZ):
        wide = parts[z].astype(F32)
        squares = squares + jnp.sum(wide * wide, axis=1, keepdims=True)
    scale = lax.rsqrt(squares * (1.0 / D) + EPSILON)
    r = lax.broadcasted_iota(jnp.int32, (16, 16), 0)
    c = lax.broadcasted_iota(jnp.int32, (16, 16), 1)
    pick = jnp.where((c == info[4] * FINE + r) & (r < FINE), 1.0, 0.0).astype(BF16)
    for z in range(NZ):
        place = slice(z * COLS, (z + 1) * COLS)
        mid = parts[z]
        normed = (mid.astype(F32) * scale * gain[:, place].astype(F32)).astype(BF16)
        for e in range(NE):
            out[e, :, place] = normed
        own[:, place] = jnp.dot(pick, mid, preferred_element_type=F32).astype(BF16)


MOE_PIECES = 4
MOE_TILE = D // MOE_PIECES


def moe_kernel(info, x, ids, router, *refs):
    sources, out, held, sems = refs[:6], refs[6], refs[7:13], refs[13]
    units = sources[0].shape[1]
    copies = []
    for k in range(2 * MOE_PIECES):
        place = pl.ds(k % MOE_PIECES * MOE_TILE, MOE_TILE)
        group = range(4) if k < MOE_PIECES else range(4, 6)
        copies.append([])
        for i in group:
            at = (place, slice(None)) if i < 4 else (slice(None), place)
            copy = pltpu.make_async_copy(sources[i].at[at], held[i].at[at], sems.at[k, i % 4])
            copy.start()
            copies[k].append(copy)

    core, expert = info[2], info[5]
    rows = x[...].reshape(128, D)
    logits = lax.dot_general(
        rows, router[...], (((1,), (1,)), ((), ())), preferred_element_type=F32
    )
    r = lax.broadcasted_iota(jnp.int32, (128, SPAN), 0)
    u = lax.broadcasted_iota(jnp.int32, (128, SPAN), 1)
    token = (r % 16 // FINE * 2 + core) * BLOCK_TOKENS + r // 16 * FINE + r % FINE
    leading, trailing = ids[0:1, :], ids[1:2, :]
    chosen = (leading == expert) | (trailing == expert)
    other = jnp.where(leading == expert, trailing, leading)
    earlier = jnp.sum(jnp.where(chosen & (u < token), 1.0, 0.0), axis=1, keepdims=True)
    mine = jnp.sum(jnp.where(chosen & (u == token), 1.0, 0.0), axis=1, keepdims=True)
    other_id = jnp.sum(jnp.where(u == token, other.astype(F32), 0.0), axis=1, keepdims=True)
    lane = lax.broadcasted_iota(jnp.int32, logits.shape, 1)
    own_logit = jnp.sum(jnp.where(lane == expert, logits, 0.0), axis=1, keepdims=True)
    other_logit = jnp.sum(
        jnp.where(lane.astype(F32) == other_id, logits, 0.0), axis=1, keepdims=True
    )
    active = (mine > 0.5) & (earlier < CAP - 0.5)
    share = jnp.where(active, 1.0 / (1.0 + jnp.exp(other_logit - own_logit)), 0.0)

    sums = [jnp.zeros((128, units), F32)] * 4
    for k in range(MOE_PIECES):
        for copy in copies[k]:
            copy.wait()
        place = slice(k * MOE_TILE, (k + 1) * MOE_TILE)
        part = x[:, :, place].reshape(128, MOE_TILE)
        sums = [
            sums[i] + jnp.dot(part, held[i][place, :], preferred_element_type=F32) for i in range(4)
        ]
    hidden = [
        (sums[i] / (1.0 + jnp.exp(-sums[i])) * sums[i + 2]).astype(BF16) for i in range(2)
    ]
    for k in range(MOE_PIECES):
        for copy in copies[MOE_PIECES + k]:
            copy.wait()
        place = slice(k * MOE_TILE, (k + 1) * MOE_TILE)
        total = jnp.dot(hidden[0], held[4][:, place], preferred_element_type=F32)
        total = total + jnp.dot(hidden[1], held[5][:, place], preferred_element_type=F32)
        out[:, :, place] = (total * share).astype(BF16).reshape(NE, 16, MOE_TILE)


def experts(info, x, ids, router, *weights):
    units = weights[0].shape[1]
    return call(
        moe_kernel,
        (NE, 16, D),
        info,
        x,
        ids,
        router,
        *[in_hbm(w) for w in weights],
        specs=[SMEM] + [VMEM] * 3 + [ANY] * 6,
        limit=40,
        flops=6 * 128 * D * 512,
        scratch=[pltpu.VMEM((D, units), BF16)] * 4
        + [pltpu.VMEM((units, D), BF16)] * 2
        + [pltpu.SemaphoreType.DMA((2 * MOE_PIECES, 4))],
    )


def sum_kernel(parts, out):
    total = parts[0].astype(F32)
    for e in range(1, NE):
        total = total + parts[e].astype(F32)
    for z in range(NZ):
        out[z] = total[z * FINE : (z + 1) * FINE].astype(BF16)


def last_kernel(parts, own, out):
    total = own[:, :].astype(F32)[:FINE]
    for z in range(NZ):
        total = total + parts[z].astype(F32)
    out[...] = total.astype(BF16)


def shards(
    queries,
    span_keys,
    span_values,
    cache_keys,
    cache_values,
    span_start,
    residual,
    out_weight,
    norm_gain,
    router_weight,
    expert_ids,
    gate_weight,
    up_weight,
    down_weight,
):
    ctx_index = lax.axis_index("ctx")
    core = ctx_index % 2
    z_index = ctx_index // 2
    key_rows = cache_keys.shape[0]

    other_keys = sibling(cache_keys)
    other_values = sibling(cache_values)
    span_own = jnp.concatenate([span_keys, span_values], axis=1)
    other_span = sibling(span_own)
    message = call(
        first_message_kernel,
        (NZ, MESSAGE_ROWS, HEAD_DIM),
        in_hbm(queries),
        in_hbm(residual),
        space=pltpu.HBM,
    )
    first = exchange_z(message)
    other_out = sibling(out_weight)
    other_gate = sibling(gate_weight)
    other_up = sibling(up_weight)
    other_down = sibling(down_weight)

    def valid(index):
        return jnp.clip(span_start[0] - index * key_rows, 0, key_rows)

    own_first = core == 0
    span_both = jnp.concatenate(
        [jnp.where(own_first, span_own, other_span), jnp.where(own_first, other_span, span_own)], axis=0
    )
    info = jnp.stack(
        [
            valid(ctx_index),
            valid(ctx_index ^ 1),
            core,
            z_index * 2 * BLOCK_TOKENS,
            z_index,
            z_index // 2,
        ]
    ).astype(jnp.int32)
    prepared_values, prepared_keys = prepare(in_hbm(cache_values), other_values, other_keys)
    partial = call(
        attention_kernel,
        (NZ, MESSAGE_ROWS, HEAD_DIM),
        info,
        first,
        in_hbm(cache_keys),
        in_hbm(prepared_keys),
        in_hbm(prepared_values),
        span_both[:, :HEAD_DIM],
        span_both[:, HEAD_DIM:],
        specs=[SMEM, VMEM, ANY, ANY, ANY, VMEM, VMEM],
        space=pltpu.HBM,
        limit=48,
        flops=64 * ROWS * 2 * CHUNK * HEAD_DIM,
        scratch=[
            pltpu.VMEM((ROWS, HEAD_DIM), BF16),
            pltpu.VMEM((2, CHUNK, HEAD_DIM), BF16),
            pltpu.VMEM((2, HEAD_DIM + 16, CHUNK), BF16),
            pltpu.VMEM((8, ROWS), F32),
            pltpu.VMEM((HEAD_DIM + 16, ROWS), F32),
            pltpu.SemaphoreType.DMA((4,)),
            pltpu.SMEM((1,), jnp.int32),
        ],
    )
    second = exchange_z(partial)
    attended, other_out, gain = call_and_pass(
        combine_kernel,
        (NZ, BLOCK_TOKENS, COLS),
        (second,),
        (in_vmem(other_out), in_hbm(norm_gain.reshape(1, D))),
    )
    third = exchange_z(attended)
    fourth = exchange_exp(
        call(
            project_kernel,
            (NE, 16, COLS),
            info,
            third,
            out_weight,
            other_out,
            specs=[SMEM, VMEM, VMEM, VMEM],
        )
    )
    fifth = exchange_z(call(mid_kernel, (NZ, 16, COLS), fourth, first))
    passed = [in_hbm(w) for w in (other_gate, other_up, other_down)]
    normed, own_mid, other_gate, other_up, other_down = pl.pallas_call(
        norm_kernel,
        out_shape=[
            jax.ShapeDtypeStruct((NE, 16, D), BF16),
            jax.ShapeDtypeStruct((16, D), BF16),
        ]
        + [jax.ShapeDtypeStruct(w.shape, w.dtype) for w in passed],
        in_specs=[SMEM, VMEM, VMEM, ANY, ANY, ANY],
        out_specs=[VMEM, VMEM, ANY, ANY, ANY],
        input_output_aliases={3: 2, 4: 3, 5: 4},
        compiler_params=pltpu.CompilerParams(vmem_limit_bytes=16 << 20),
        cost_estimate=pl.CostEstimate(flops=1 << 20, bytes_accessed=2 << 20, transcendentals=0),
    )(info, fifth, gain, *passed)
    tokens = exchange_exp(normed)

    result = experts(
        info,
        tokens,
        expert_ids.T,
        router_weight.T,
        gate_weight,
        other_gate,
        up_weight,
        other_up,
        down_weight,
        other_down,
    )
    sixth = exchange_exp(result)
    seventh = exchange_z(call(sum_kernel, (NZ, FINE, D), sixth))
    return call(last_kernel, (FINE, D), seventh, own_mid)


def solution(mesh):
    placed = (
        P(("dp", "ctx"), "exp"),
        P(("dp", "ctx"), "exp"),
        P(("dp", "ctx"), "exp"),
        P(("dp", "ctx"), "exp"),
        P(("dp", "ctx"), "exp"),
        P("dp"),
        P(("dp", "ctx", "exp"), None),
        P("exp", "ctx"),
        P(),
        P(),
        P("dp", None),
        P(None, ("ctx", "exp")),
        P(None, ("ctx", "exp")),
        P(("ctx", "exp"), None),
    )
    return jax.shard_map(
        shards, mesh=mesh, in_specs=placed, out_specs=P(("dp", "ctx", "exp"), None), check_vma=False
    )
```

profile of v0, /device:TPU:2, one launch (start us, length us, event | category | flops | bytes accessed | tf_op | source)
XLA Modules:
  0.0 155.2 jit_solution(5098442829165030418)
XLA Ops:
  0.0 0.0 collective-permute-start.1
  0.0 0.5 collective-permute-start
  0.5 1.5 shard_map.136
  2.0 8.5 %all-to-all-start = ((bf16[8,112,128]{2,1,0:T(8,128)(2,1)}), bf16[8,112,128]{2,1,0:T(8,128)(2,1)S(1)}, u32[]{:S(2)}, u32[]{:S(2)}) async-start(bf16[8,112,128]{2,1,0:T(8,128)(2,1)} %shard_map.136), calls=%async_computation | async-start | bytes 458752 | tf_op jit(solution)/shard_map/all_to_all | solution.py:42
  10.5 0.7 constant_dynamic-update-slice_fusion.1
  11.2 0.7 constant_dynamic-update-slice_fusion
  11.9 0.0 collective-permute-start.2
  11.9 0.5 collective-permute-start.3
  12.4 0.0 collective-permute-start.4
  13.1 0.1 stack.27.info
  13.1 0.0 collective-permute-done.2
  13.1 0.6 collective-permute-start.5
  13.7 0.0 collective-permute-done.1.k1
  13.7 0.1 collective-permute-start.6
  13.8 0.0 collective-permute-done.v1
  13.9 3.6 %shard_map.137 = (bf16[2,144,4096]{2,1,0:T(8,128)(2,1)}, bf16[4096,128]{1,0:T(8,128)(2,1)}) custom-call(bf16[4096,128]{1,0:T(8,128)(2,1)} %v0.1, bf16[4096,128]{1,0:T(8,128)(2,1)S(1)} %collective-permute-done.v1, bf16[4096,128]{1,0:T(8,128)(2,1)S(1)} %collective-permute-done.1.k1), custom_call_target="tpu_custom_call" | custom-call | bytes 6291456 | tf_op jit(solution)/shard_map/pallas_call | solution.py:121
  17.5 4.3 %all-to-all-done.first.message = bf16[8,112,128]{2,1,0:T(8,128)(2,1)S(1)} async-done(((bf16[8,112,128]{2,1,0:T(8,128)(2,1)}), bf16[8,112,128]{2,1,0:T(8,128)(2,1)S(1)}, u32[]{:S(2)}, u32[]{:S(2)}) %all-to-all-start) | async-done | bytes 229408 | tf_op jit(solution)/shard_map/all_to_all | solution.py:42
  21.8 0.0 copy-start.4
  21.8 0.0 copy-start
  21.8 10.3 %shard_map.138 = bf16[8,112,128]{2,1,0:T(8,128)(2,1)} custom-call(s32[6]{0:T(128)S(1)} %stack.27.info, bf16[8,112,128]{2,1,0:T(8,128)(2,1)S(1)} %all-to-all-done.first.message, bf16[4096,128]{1,0:T(8,128)(2,1)} %k0.1, bf16[4096,128]{1,0:T(8,128)(2,1)} %get-tuple-element.15.k1, bf16[2,144,4096]{2,1,0:T(8,128)(2,1)} %get-tuple-element.16.turned, ...), custom_call_target="tpu_custom_call" | custom-call | flops 51539607552 | bytes 1048576 | tf_op jit(solution)/shard_map/pallas_call | solution.py:76
  32.1 3.4 %all-to-all-start.1 = ((bf16[8,112,128]{2,1,0:T(8,128)(2,1)}), bf16[8,112,128]{2,1,0:T(8,128)(2,1)S(1)}, u32[]{:S(2)}, u32[]{:S(2)}) async-start(bf16[8,112,128]{2,1,0:T(8,128)(2,1)} %shard_map.138), calls=%async_computation.1 | async-start | bytes 458752 | tf_op jit(solution)/shard_map/all_to_all | solution.py:42
  35.6 0.0 copy-done.4
  35.6 0.6 reshape.3.refs_1_
  36.2 0.0 collective-permute-done.3.refs_0_
  36.2 9.4 %all-to-all-done.1.message = bf16[8,112,128]{2,1,0:T(8,128)(2,1)S(1)} async-done(((bf16[8,112,128]{2,1,0:T(8,128)(2,1)}), bf16[8,112,128]{2,1,0:T(8,128)(2,1)S(1)}, u32[]{:S(2)}, u32[]{:S(2)}) %all-to-all-start.1) | async-done | bytes 229408 | tf_op jit(solution)/shard_map/all_to_all | solution.py:42
  45.6 0.3 shard_map.139
  45.9 0.0 copy-start.1
  45.9 12.2 %all_to_all.40.x = bf16[8,16,768]{2,1,0:T(8,128)(2,1)S(1)} all-to-all(bf16[8,16,768]{2,1,0:T(8,128)(2,1)S(1)} %get-tuple-element.17), channel_id=1, replica_groups={{0,16,32,48,64,80,96,112},{8,24,40,56,72,88,104,120},{1,17,33,49,65,81,..., dimensions={0} | all-to-all | bytes 393216 | tf_op jit(solution)/shard_map/all_to_all | solution.py:42
  58.1 0.0 copy-done
  58.1 1.0 shard_map.140
  59.2 23.4 %all_to_all.41.parts = bf16[8,16,768]{2,1,0:T(8,128)(2,1)S(1)} all-to-all(bf16[8,16,768]{2,1,0:T(8,128)(2,1)S(1)} %shard_map.140), channel_id=1, replica_groups=mesh['dp'=2,'ctx'=16,'exp'=8] {'exp'}, dimensions={0} | all-to-all | bytes 393216 | tf_op jit(solution)/shard_map/all_to_all | solution.py:46
  82.6 0.2 shard_map.141
  82.8 12.2 %all_to_all.42.parts = bf16[8,16,768]{2,1,0:T(8,128)(2,1)S(1)} all-to-all(bf16[8,16,768]{2,1,0:T(8,128)(2,1)S(1)} %shard_map.141), channel_id=1, replica_groups={{0,16,32,48,64,80,96,112},{8,24,40,56,72,88,104,120},{1,17,33,49,65,81,..., dimensions={0} | all-to-all | bytes 393216 | tf_op jit(solution)/shard_map/all_to_all | solution.py:42
  94.9 0.0 collective-permute-done.4.refs_0_
  94.9 0.0 collective-permute-done.5.refs_1_
  94.9 0.0 collective-permute-done.6.refs_2_
  95.0 0.0 copy-done.1
  95.0 0.8 shard_map.142
  95.8 0.0 copy-start.2
  95.8 0.0 copy-start.3
  95.8 19.4 %all_to_all.43.x = bf16[8,16,6144]{2,1,0:T(8,128)(2,1)S(1)} all-to-all(bf16[8,16,6144]{2,1,0:T(8,128)(2,1)S(1)} %get-tuple-element.20), channel_id=1, replica_groups=mesh['dp'=2,'ctx'=16,'exp'=8] {'exp'}, dimensions={0} | all-to-all | bytes 3145728 | tf_op jit(solution)/shard_map/all_to_all | solution.py:46
  115.2 0.0 copy-done.2
  115.2 0.0 copy-done.3
  115.2 8.4 %shard_map.143 = bf16[8,16,6144]{2,1,0:T(8,128)(2,1)S(1)} custom-call(s32[6]{0:T(128)S(1)} %stack.27.info, bf16[8,16,6144]{2,1,0:T(8,128)(2,1)S(1)} %all_to_all.43.x, s32[2,256]{1,0:T(2,128)S(1)} %bitcast.12, bf16[4,6144]{1,0:T(4,128)(2,1)S(1)} %bitcast.11, bf16[6144,256]{1,0:T(8,128)(2,1)} %refs_0_.1, bf16[6144,256]{1,0:T(8,128)(2,1)} %get-tuple-element.21.refs_1_, ...), custom_call_target="tpu_custom_call" | custom-call | flops 2415919104 | bytes 1048576 | tf_op jit(solution)/shard_map/pallas_call | solution.py:76
  123.6 18.4 %all_to_all.44.parts = bf16[8,16,6144]{2,1,0:T(8,128)(2,1)S(1)} all-to-all(bf16[8,16,6144]{2,1,0:T(8,128)(2,1)S(1)} %shard_map.143), channel_id=1, replica_groups=mesh['dp'=2,'ctx'=16,'exp'=8] {'exp'}, dimensions={0} | all-to-all | bytes 3145728 | tf_op jit(solution)/shard_map/all_to_all | solution.py:46
  142.0 0.2 shard_map.144
  142.3 12.2 %all_to_all.45.parts = bf16[8,2,6144]{2,1,0:T(2,128)(2,1)S(1)} all-to-all(bf16[8,2,6144]{2,1,0:T(2,128)(2,1)S(1)} %shard_map.144), channel_id=1, replica_groups={{0,16,32,48,64,80,96,112},{8,24,40,56,72,88,104,120},{1,17,33,49,65,81,..., dimensions={0} | all-to-all | bytes 393216 | tf_op jit(solution)/shard_map/all_to_all | solution.py:42
  154.4 0.8 shard_map.145
  (2 shorter events, 0.0 us)
Async XLA Ops:
  0.0 13.7 %collective-permute-start.1 = (bf16[4096,128]{1,0:T(8,128)(2,1)}, bf16[4096,128]{1,0:T(8,128)(2,1)S(1)}, u32[]{:S(2)}, u32[]{:S(2)}) collective-permute-start(bf16[4096,128]{1,0:T(8,128)(2,1)} %k0.1), channel_id=1, source_target_pairs={{0,8},{8,0},{16,24},{24,16},{32,40},{40,32},{48,56},{56,48},{64,72... | collective-permute-start | bytes 3145736 | tf_op jit(solution)/shard_map/ppermute | solution.py:50
  0.0 13.8 %collective-permute-start = (bf16[4096,128]{1,0:T(8,128)(2,1)}, bf16[4096,128]{1,0:T(8,128)(2,1)S(1)}, u32[]{:S(2)}, u32[]{:S(2)}) collective-permute-start(bf16[4096,128]{1,0:T(8,128)(2,1)} %v0.1), channel_id=1, source_target_pairs={{0,8},{8,0},{16,24},{24,16},{32,40},{40,32},{48,56},{56,48},{64,72... | collective-permute-start | bytes 3145736 | tf_op jit(solution)/shard_map/ppermute | solution.py:50
  2.0 19.8 %all-to-all-start = ((bf16[8,112,128]{2,1,0:T(8,128)(2,1)}), bf16[8,112,128]{2,1,0:T(8,128)(2,1)S(1)}, u32[]{:S(2)}, u32[]{:S(2)}) async-start(bf16[8,112,128]{2,1,0:T(8,128)(2,1)} %shard_map.136), calls=%async_computation | async-start | bytes 458752 | tf_op jit(solution)/shard_map/all_to_all | solution.py:42
  11.9 1.3 collective-permute-start.2
  11.9 24.3 %collective-permute-start.3 = (bf16[768,384]{1,0:T(8,128)(2,1)}, bf16[768,384]{1,0:T(8,128)(2,1)S(1)}, u32[]{:S(2)}, u32[]{:S(2)}) collective-permute-start(bf16[768,384]{1,0:T(8,128)(2,1)} %own.1), channel_id=1, source_target_pairs={{0,8},{8,0},{16,24},{24,16},{32,40},{40,32},{48,56},{56,48},{64,72... | collective-permute-start | bytes 1769480 | tf_op jit(solution)/shard_map/ppermute | solution.py:50
  12.4 82.5 %collective-permute-start.4 = (bf16[6144,256]{1,0:T(8,128)(2,1)}, bf16[6144,256]{1,0:T(8,128)(2,1)}, u32[]{:S(2)}, u32[]{:S(2)}) collective-permute-start(bf16[6144,256]{1,0:T(8,128)(2,1)} %refs_0_.1), channel_id=1, source_target_pairs={{0,8},{8,0},{16,24},{24,16},{32,40},{40,32},{48,56},{56,48},{64,72... | collective-permute-start | bytes 9437192 | tf_op jit(solution)/shard_map/ppermute | solution.py:50
  13.1 81.8 %collective-permute-start.5 = (bf16[6144,256]{1,0:T(8,128)(2,1)}, bf16[6144,256]{1,0:T(8,128)(2,1)}, u32[]{:S(2)}, u32[]{:S(2)}) collective-permute-start(bf16[6144,256]{1,0:T(8,128)(2,1)} %refs_2_.1), channel_id=1, source_target_pairs={{0,8},{8,0},{16,24},{24,16},{32,40},{40,32},{48,56},{56,48},{64,72... | collective-permute-start | bytes 9437192 | tf_op jit(solution)/shard_map/ppermute | solution.py:50
  13.7 81.2 %collective-permute-start.6 = (bf16[256,6144]{1,0:T(8,128)(2,1)}, bf16[256,6144]{1,0:T(8,128)(2,1)}, u32[]{:S(2)}, u32[]{:S(2)}) collective-permute-start(bf16[256,6144]{1,0:T(8,128)(2,1)} %refs_4_.1), channel_id=1, source_target_pairs={{0,8},{8,0},{16,24},{24,16},{32,40},{40,32},{48,56},{56,48},{64,72... | collective-permute-start | bytes 9437192 | tf_op jit(solution)/shard_map/ppermute | solution.py:50
  21.8 13.7 %copy-start.4 = (bf16[6144]{0:T(1024)(128)(2,1)S(1)}, bf16[6144]{0:T(1024)(128)(2,1)}, u32[]{:S(2)}) copy-start(bf16[6144]{0:T(1024)(128)(2,1)} %param.22) | copy-start | bytes 36868
  21.8 36.3 %copy-start = (bf16[768,384]{1,0:T(8,128)(2,1)S(1)}, bf16[768,384]{1,0:T(8,128)(2,1)}, u32[]{:S(2)}) copy-start(bf16[768,384]{1,0:T(8,128)(2,1)} %own.1) | copy-start | bytes 1769476
  32.1 13.5 %all-to-all-start.1 = ((bf16[8,112,128]{2,1,0:T(8,128)(2,1)}), bf16[8,112,128]{2,1,0:T(8,128)(2,1)S(1)}, u32[]{:S(2)}, u32[]{:S(2)}) async-start(bf16[8,112,128]{2,1,0:T(8,128)(2,1)} %shard_map.138), calls=%async_computation.1 | async-start | bytes 458752 | tf_op jit(solution)/shard_map/all_to_all | solution.py:42
  45.9 49.0 %copy-start.1 = (bf16[1,6144]{1,0:T(2,128)(2,1)S(1)}, bf16[1,6144]{1,0:T(2,128)(2,1)}, u32[]{:S(2)}) copy-start(bf16[1,6144]{1,0:T(2,128)(2,1)} %get-tuple-element.19.gain) | copy-start | bytes 36868
  95.8 19.4 %copy-start.2 = (bf16[6144,4]{0,1:T(4,128)(2,1)S(1)}, bf16[6144,4]{0,1:T(4,128)(2,1)}, u32[]{:S(2)}) copy-start(bf16[6144,4]{0,1:T(4,128)(2,1)} %param.23) | copy-start | bytes 147460
  95.8 19.4 %copy-start.3 = (s32[256,2]{0,1:T(2,128)S(1)}, s32[256,2]{0,1:T(2,128)}, u32[]{:S(2)}) copy-start(s32[256,2]{0,1:T(2,128)} %param.24) | copy-start | bytes 6148
where the time goes:
time: 157 us; the launch traced here: 155 us
  blocking collectives  97.8 us (62%)
  Pallas kernels  27.1 us (17%)
  waiting for transfers between devices  13.8 us (9%)
  starting transfers between devices  13.6 us (9%)
  local copies, waits for them, and re-layouts  2.11 us (1%)
    all_to_all x3, blocking collectives, exchange_exp(): return lax.all_to_all(blocks, 'exp', 0, 0, tiled=True)  61.3 us
    all_to_all x3, blocking collectives, exchange_z(): lax.all_to_all(blocks, 'ctx', 0, 0, axis_index_groups=Z_GROUPS, tiled=True)  36.5 us
    pallas_call x7, Pallas kernels, call(): pl.pallas_call(kernel, out_shape=space(shape, BF16), in_specs=specs or [V...  22.4 us
    all_to_all x2, waiting for transfers between devices, exchange_z(): lax.all_to_all(blocks, 'ctx', 0, 0, axis_index_groups=Z_GROUPS, tiled=True)  13.8 us
    all_to_all x2, starting transfers between devices, exchange_z(): lax.all_to_all(blocks, 'ctx', 0, 0, axis_index_groups=Z_GROUPS, tiled=True)  11.9 us
    pallas_call x1, Pallas kernels, prepare(): pl.pallas_call(prepare_kernel, out_shape=(pltpu.HBM((2, HEAD_DIM + 16, CH...  3.63 us
  transfers between devices with their start and end apart: 9, of which 2 were waited for; matrix products, arithmetic and copies ran while one was open for 1% of the time, Pallas kernels for 11%

commit v1 on v0

--- a/solution.py
+++ b/solution.py
@@ -84,7 +84,9 @@
     )(*args)
 
 
-def first_message_kernel(q, residual, out):
+def first_message_kernel(q, residual, span_keys, span_values, out, span):
+    span[:, :HEAD_DIM] = span_keys[...]
+    span[:, HEAD_DIM:] = span_values[...]
     res = residual[...].astype(F32)
     row = lax.broadcasted_iota(jnp.int32, (16, HEAD_DIM), 0)
     for z in range(NZ):
@@ -156,15 +158,21 @@
 
     core = info[2]
     span_rows = 2 * BLOCK_TOKENS
+    mine, theirs = sk[...].astype(F32), sv[...].astype(F32)
+    lead = (core == 0).astype(F32)
+    pair = jnp.concatenate(
+        [mine * lead + theirs * (1.0 - lead), theirs * lead + mine * (1.0 - lead)], axis=0
+    ).astype(BF16)
+    key_pair, value_pair = pair[:, :HEAD_DIM], pair[:, HEAD_DIM:]
 
     def begin():
-        span_values = jnp.concatenate([sv[...].T, jnp.ones((16, span_rows), BF16)], axis=0)
+        span_values = jnp.concatenate([value_pair.T, jnp.ones((16, span_rows), BF16)], axis=0)
         for b in range(blocks):
             row = lax.broadcasted_iota(jnp.int32, (span_rows, Q_BLOCK), 0)
             col = lax.broadcasted_iota(jnp.int32, (span_rows, Q_BLOCK), 1) + b * Q_BLOCK
             token = col // BLOCK_ROWS * span_rows + core * BLOCK_TOKENS + col % BLOCK_TOKENS
             allowed = info[3] + row <= token
-            s = jnp.where(allowed, scores_of(sk[...], b), MASKED)
+            s = jnp.where(allowed, scores_of(key_pair, b), MASKED)
             top = jnp.max(s, axis=0, keepdims=True)
             w = jnp.where(allowed, jnp.exp2((s - top) * EXP2_SCALE), 0.0).astype(BF16)
             peak[:, columns(b)] = jnp.broadcast_to(top, (8, Q_BLOCK))
@@ -203,11 +211,12 @@
             carried[:, columns(b)] = (held if factor is None else held * factor) + sums
 
         wait(0)
-        s = scores(items[0])
+        s, later = scores(items[0]), scores(items[1])
         wait(1)
         earlier = None
         for i, item in enumerate(items):
-            later = scores(items[i + 1]) if i + 1 < len(items) else None
+            if i > 0:
+                later = scores(items[i + 1]) if i + 1 < len(items) else None
             current = soften_near(s, item[1], item[0]) if near else soften(s, item[1])
             if earlier is not None:
                 gather(items[i - 1], *earlier)
@@ -476,15 +485,18 @@
 
     other_keys = sibling(cache_keys)
     other_values = sibling(cache_values)
-    span_own = jnp.concatenate([span_keys, span_values], axis=1)
+    message, span_own = pl.pallas_call(
+        first_message_kernel,
+        out_shape=(
+            pltpu.HBM((NZ, MESSAGE_ROWS, HEAD_DIM), BF16),
+            jax.ShapeDtypeStruct((BLOCK_TOKENS, 2 * HEAD_DIM), BF16),
+        ),
+        in_specs=[VMEM] * 4,
+        out_specs=(VMEM, VMEM),
+        compiler_params=pltpu.CompilerParams(vmem_limit_bytes=32 << 20),
+        cost_estimate=pl.CostEstimate(flops=1 << 20, bytes_accessed=1 << 20, transcendentals=0),
+    )(in_hbm(queries), in_hbm(residual), in_hbm(span_keys), in_hbm(span_values))
     other_span = sibling(span_own)
-    message = call(
-        first_message_kernel,
-        (NZ, MESSAGE_ROWS, HEAD_DIM),
-        in_hbm(queries),
-        in_hbm(residual),
-        space=pltpu.HBM,
-    )
     first = exchange_z(message)
     other_out = sibling(out_weight)
     other_gate = sibling(gate_weight)
@@ -494,10 +506,6 @@
     def valid(index):
         return jnp.clip(span_start[0] - index * key_rows, 0, key_rows)
 
-    own_first = core == 0
-    span_both = jnp.concatenate(
-        [jnp.where(own_first, span_own, other_span), jnp.where(own_first, other_span, span_own)], axis=0
-    )
     info = jnp.stack(
         [
             valid(ctx_index),
@@ -517,8 +525,8 @@
         in_hbm(cache_keys),
         in_hbm(prepared_keys),
         in_hbm(prepared_values),
-        span_both[:, :HEAD_DIM],
-        span_both[:, HEAD_DIM:],
+        span_own,
+        other_span,
         specs=[SMEM, VMEM, ANY, ANY, ANY, VMEM, VMEM],
         space=pltpu.HBM,
         limit=48,

time: 157 us -> 157 us (level); the launches traced: 155 us -> 157 us
  blocking collectives: 97.8 us -> 99.9 us
    all_to_all x3, blocking collectives: 61.3 us -> 63.4 us  [exchange_exp(): return lax.all_to_all(blocks, 'exp', 0, 0, tiled=True)]
    pallas_call x7 -> x6, Pallas kernels: 22.4 us -> 20.7 us  [call(): pl.pallas_call(kernel, out_shape=space(shape, BF16), in_specs=specs or [V...]
  transfers between devices with their start and end apart: 9 -> 9, of which waited for: 2 -> 2; matrix products, arithmetic and copies ran while one was open for 1% -> 0% of each run, Pallas kernels for 11% -> 11%
where the time goes in v1:
time: 157 us
  blocking collectives  99.9 us (64%)
  Pallas kernels  27 us (17%)
  waiting for transfers between devices  15.2 us (10%)
  starting transfers between devices  13.6 us (9%)
    all_to_all x3, blocking collectives, exchange_exp(): return lax.all_to_all(blocks, 'exp', 0, 0, tiled=True)  63.4 us
    all_to_all x3, blocking collectives, exchange_z(): lax.all_to_all(blocks, 'ctx', 0, 0, axis_index_groups=Z_GROUPS, tiled=True)  36.5 us
    pallas_call x6, Pallas kernels, call(): pl.pallas_call(kernel, out_shape=space(shape, BF16), in_specs=specs or [V...  20.7 us
    all_to_all x2, waiting for transfers between devices, exchange_z(): lax.all_to_all(blocks, 'ctx', 0, 0, axis_index_groups=Z_GROUPS, tiled=True)  15.2 us
    all_to_all x2, starting transfers between devices, exchange_z(): lax.all_to_all(blocks, 'ctx', 0, 0, axis_index_groups=Z_GROUPS, tiled=True)  11.9 us
    pallas_call x1, Pallas kernels, prepare(): pl.pallas_call(prepare_kernel, out_shape=(pltpu.HBM((2, HEAD_DIM + 16, CH...  3.62 us
  transfers between devices with their start and end apart: 9, of which 2 were waited for; matrix products, arithmetic and copies ran while one was open for 0% of the time, Pallas kernels for 11%

profile of v1, /device:TPU:2, one launch (start us, length us, event | category | flops | bytes accessed | tf_op | source)
XLA Modules:
  0.0 157.2 jit_solution(1635033816094569332)
XLA Ops:
  0.0 0.0 collective-permute-start.1
  0.0 0.5 collective-permute-start
  0.5 1.5 shard_map.136
  2.0 8.5 %all-to-all-start = ((bf16[8,112,128]{2,1,0:T(8,128)(2,1)}), bf16[8,112,128]{2,1,0:T(8,128)(2,1)S(1)}, u32[]{:S(2)}, u32[]{:S(2)}) async-start(bf16[8,112,128]{2,1,0:T(8,128)(2,1)} %get-tuple-element.17), calls=%async_computation | async-start | bytes 458752 | tf_op jit(solution)/shard_map/all_to_all | solution.py:42
  10.5 0.0 collective-permute-start.2
  10.5 0.5 collective-permute-start.3
  11.0 0.1 collective-permute-start.4
  11.8 0.1 stack.27.info
  11.9 0.0 collective-permute-done.1.k1
  11.9 0.5 collective-permute-start.5
  12.3 0.0 collective-permute-done.v1
  12.3 0.1 collective-permute-start.6
  12.4 3.6 %shard_map.137 = (bf16[2,144,4096]{2,1,0:T(8,128)(2,1)}, bf16[4096,128]{1,0:T(8,128)(2,1)}) custom-call(bf16[4096,128]{1,0:T(8,128)(2,1)} %v0.1, bf16[4096,128]{1,0:T(8,128)(2,1)S(1)} %collective-permute-done.v1, bf16[4096,128]{1,0:T(8,128)(2,1)S(1)} %collective-permute-done.1.k1), custom_call_target="tpu_custom_call" | custom-call | bytes 6291456 | tf_op jit(solution)/shard_map/pallas_call | solution.py:123
  16.1 0.0 collective-permute-done.2.sv
  16.1 5.8 %all-to-all-done.first.message = bf16[8,112,128]{2,1,0:T(8,128)(2,1)S(1)} async-done(((bf16[8,112,128]{2,1,0:T(8,128)(2,1)}), bf16[8,112,128]{2,1,0:T(8,128)(2,1)S(1)}, u32[]{:S(2)}, u32[]{:S(2)}) %all-to-all-start) | async-done | bytes 229408 | tf_op jit(solution)/shard_map/all_to_all | solution.py:42
  21.8 0.0 copy-start.4
  21.9 0.0 copy-start
  21.9 10.1 %shard_map.138 = bf16[8,112,128]{2,1,0:T(8,128)(2,1)} custom-call(s32[6]{0:T(128)S(1)} %stack.27.info, bf16[8,112,128]{2,1,0:T(8,128)(2,1)S(1)} %all-to-all-done.first.message, bf16[4096,128]{1,0:T(8,128)(2,1)} %k0.1, bf16[4096,128]{1,0:T(8,128)(2,1)} %get-tuple-element.18.k1, bf16[2,144,4096]{2,1,0:T(8,128)(2,1)} %get-tuple-element.19.turned, ...), custom_call_target="tpu_custom_call" | custom-call | flops 51539607552 | bytes 1048576 | tf_op jit(solution)/shard_map/pallas_call | solution.py:76
  32.0 3.4 %all-to-all-start.1 = ((bf16[8,112,128]{2,1,0:T(8,128)(2,1)}), bf16[8,112,128]{2,1,0:T(8,128)(2,1)S(1)}, u32[]{:S(2)}, u32[]{:S(2)}) async-start(bf16[8,112,128]{2,1,0:T(8,128)(2,1)} %shard_map.138), calls=%async_computation.1 | async-start | bytes 458752 | tf_op jit(solution)/shard_map/all_to_all | solution.py:42
  35.4 0.0 copy-done.4
  35.4 0.6 reshape.3.refs_1_
  36.0 0.0 collective-permute-done.3.refs_0_
  36.0 9.4 %all-to-all-done.1.message = bf16[8,112,128]{2,1,0:T(8,128)(2,1)S(1)} async-done(((bf16[8,112,128]{2,1,0:T(8,128)(2,1)}), bf16[8,112,128]{2,1,0:T(8,128)(2,1)S(1)}, u32[]{:S(2)}, u32[]{:S(2)}) %all-to-all-start.1) | async-done | bytes 229408 | tf_op jit(solution)/shard_map/all_to_all | solution.py:42
  45.5 0.3 shard_map.139
  45.8 0.0 copy-start.1
  45.8 12.2 %all_to_all.40.x = bf16[8,16,768]{2,1,0:T(8,128)(2,1)S(1)} all-to-all(bf16[8,16,768]{2,1,0:T(8,128)(2,1)S(1)} %get-tuple-element.21), channel_id=1, replica_groups={{0,16,32,48,64,80,96,112},{8,24,40,56,72,88,104,120},{1,17,33,49,65,81,..., dimensions={0} | all-to-all | bytes 393216 | tf_op jit(solution)/shard_map/all_to_all | solution.py:42
  58.0 0.0 copy-done
  58.0 1.0 shard_map.140
  59.0 23.9 %all_to_all.41.parts = bf16[8,16,768]{2,1,0:T(8,128)(2,1)S(1)} all-to-all(bf16[8,16,768]{2,1,0:T(8,128)(2,1)S(1)} %shard_map.140), channel_id=1, replica_groups=mesh['dp'=2,'ctx'=16,'exp'=8] {'exp'}, dimensions={0} | all-to-all | bytes 393216 | tf_op jit(solution)/shard_map/all_to_all | solution.py:46
  82.9 0.2 shard_map.141
  83.1 12.2 %all_to_all.42.parts = bf16[8,16,768]{2,1,0:T(8,128)(2,1)S(1)} all-to-all(bf16[8,16,768]{2,1,0:T(8,128)(2,1)S(1)} %shard_map.141), channel_id=1, replica_groups={{0,16,32,48,64,80,96,112},{8,24,40,56,72,88,104,120},{1,17,33,49,65,81,..., dimensions={0} | all-to-all | bytes 393216 | tf_op jit(solution)/shard_map/all_to_all | solution.py:42
  95.2 0.0 collective-permute-done.4.refs_0_
  95.2 0.0 collective-permute-done.5.refs_1_
  95.2 0.0 collective-permute-done.6.refs_2_
  95.3 0.0 copy-done.1
  95.3 0.8 shard_map.142
  96.1 0.0 copy-start.2
  96.1 0.0 copy-start.3
  96.1 20.3 %all_to_all.43.x = bf16[8,16,6144]{2,1,0:T(8,128)(2,1)S(1)} all-to-all(bf16[8,16,6144]{2,1,0:T(8,128)(2,1)S(1)} %get-tuple-element.24), channel_id=1, replica_groups=mesh['dp'=2,'ctx'=16,'exp'=8] {'exp'}, dimensions={0} | all-to-all | bytes 3145728 | tf_op jit(solution)/shard_map/all_to_all | solution.py:46
  116.4 0.0 copy-done.2
  116.4 0.0 copy-done.3
  116.4 8.4 %shard_map.143 = bf16[8,16,6144]{2,1,0:T(8,128)(2,1)S(1)} custom-call(s32[6]{0:T(128)S(1)} %stack.27.info, bf16[8,16,6144]{2,1,0:T(8,128)(2,1)S(1)} %all_to_all.43.x, s32[2,256]{1,0:T(2,128)S(1)} %bitcast.12, bf16[4,6144]{1,0:T(4,128)(2,1)S(1)} %bitcast.11, bf16[6144,256]{1,0:T(8,128)(2,1)} %refs_0_.1, bf16[6144,256]{1,0:T(8,128)(2,1)} %get-tuple-element.25.refs_1_, ...), custom_call_target="tpu_custom_call" | custom-call | flops 2415919104 | bytes 1048576 | tf_op jit(solution)/shard_map/pallas_call | solution.py:76
  124.8 19.2 %all_to_all.44.parts = bf16[8,16,6144]{2,1,0:T(8,128)(2,1)S(1)} all-to-all(bf16[8,16,6144]{2,1,0:T(8,128)(2,1)S(1)} %shard_map.143), channel_id=1, replica_groups=mesh['dp'=2,'ctx'=16,'exp'=8] {'exp'}, dimensions={0} | all-to-all | bytes 3145728 | tf_op jit(solution)/shard_map/all_to_all | solution.py:46
  144.0 0.2 shard_map.144
  144.3 12.2 %all_to_all.45.parts = bf16[8,2,6144]{2,1,0:T(2,128)(2,1)S(1)} all-to-all(bf16[8,2,6144]{2,1,0:T(2,128)(2,1)S(1)} %shard_map.144), channel_id=1, replica_groups={{0,16,32,48,64,80,96,112},{8,24,40,56,72,88,104,120},{1,17,33,49,65,81,..., dimensions={0} | all-to-all | bytes 393216 | tf_op jit(solution)/shard_map/all_to_all | solution.py:42
  156.4 0.8 shard_map.145
Async XLA Ops:
  0.0 11.9 %collective-permute-start.1 = (bf16[4096,128]{1,0:T(8,128)(2,1)}, bf16[4096,128]{1,0:T(8,128)(2,1)S(1)}, u32[]{:S(2)}, u32[]{:S(2)}) collective-permute-start(bf16[4096,128]{1,0:T(8,128)(2,1)} %k0.1), channel_id=1, source_target_pairs={{0,8},{8,0},{16,24},{24,16},{32,40},{40,32},{48,56},{56,48},{64,72... | collective-permute-start | bytes 3145736 | tf_op jit(solution)/shard_map/ppermute | solution.py:50
  0.0 12.3 %collective-permute-start = (bf16[4096,128]{1,0:T(8,128)(2,1)}, bf16[4096,128]{1,0:T(8,128)(2,1)S(1)}, u32[]{:S(2)}, u32[]{:S(2)}) collective-permute-start(bf16[4096,128]{1,0:T(8,128)(2,1)} %v0.1), channel_id=1, source_target_pairs={{0,8},{8,0},{16,24},{24,16},{32,40},{40,32},{48,56},{56,48},{64,72... | collective-permute-start | bytes 3145736 | tf_op jit(solution)/shard_map/ppermute | solution.py:50
  2.0 19.8 %all-to-all-start = ((bf16[8,112,128]{2,1,0:T(8,128)(2,1)}), bf16[8,112,128]{2,1,0:T(8,128)(2,1)S(1)}, u32[]{:S(2)}, u32[]{:S(2)}) async-start(bf16[8,112,128]{2,1,0:T(8,128)(2,1)} %get-tuple-element.17), calls=%async_computation | async-start | bytes 458752 | tf_op jit(solution)/shard_map/all_to_all | solution.py:42
  10.5 5.6 %collective-permute-start.2 = (bf16[16,256]{1,0:T(8,128)(2,1)S(1)}, bf16[16,256]{1,0:T(8,128)(2,1)S(1)}, u32[]{:S(2)}, u32[]{:S(2)}) collective-permute-start(bf16[16,256]{1,0:T(8,128)(2,1)S(1)} %get-tuple-element.20.sk), channel_id=1, source_target_pairs={{0,8},{8,0},{16,24},{24,16},{32,40},{40,32},{48,56},{56,48},{64,72... | collective-permute-start | bytes 24584 | tf_op jit(solution)/shard_map/ppermute | solution.py:50
  10.5 25.5 %collective-permute-start.3 = (bf16[768,384]{1,0:T(8,128)(2,1)}, bf16[768,384]{1,0:T(8,128)(2,1)S(1)}, u32[]{:S(2)}, u32[]{:S(2)}) collective-permute-start(bf16[768,384]{1,0:T(8,128)(2,1)} %own.1), channel_id=1, source_target_pairs={{0,8},{8,0},{16,24},{24,16},{32,40},{40,32},{48,56},{56,48},{64,72... | collective-permute-start | bytes 1769480 | tf_op jit(solution)/shard_map/ppermute | solution.py:50
  11.0 84.2 %collective-permute-start.4 = (bf16[6144,256]{1,0:T(8,128)(2,1)}, bf16[6144,256]{1,0:T(8,128)(2,1)}, u32[]{:S(2)}, u32[]{:S(2)}) collective-permute-start(bf16[6144,256]{1,0:T(8,128)(2,1)} %refs_0_.1), channel_id=1, source_target_pairs={{0,8},{8,0},{16,24},{24,16},{32,40},{40,32},{48,56},{56,48},{64,72... | collective-permute-start | bytes 9437192 | tf_op jit(solution)/shard_map/ppermute | solution.py:50
  11.9 83.4 %collective-permute-start.5 = (bf16[6144,256]{1,0:T(8,128)(2,1)}, bf16[6144,256]{1,0:T(8,128)(2,1)}, u32[]{:S(2)}, u32[]{:S(2)}) collective-permute-start(bf16[6144,256]{1,0:T(8,128)(2,1)} %refs_2_.1), channel_id=1, source_target_pairs={{0,8},{8,0},{16,24},{24,16},{32,40},{40,32},{48,56},{56,48},{64,72... | collective-permute-start | bytes 9437192 | tf_op jit(solution)/shard_map/ppermute | solution.py:50
  12.3 82.9 %collective-permute-start.6 = (bf16[256,6144]{1,0:T(8,128)(2,1)}, bf16[256,6144]{1,0:T(8,128)(2,1)}, u32[]{:S(2)}, u32[]{:S(2)}) collective-permute-start(bf16[256,6144]{1,0:T(8,128)(2,1)} %refs_4_.1), channel_id=1, source_target_pairs={{0,8},{8,0},{16,24},{24,16},{32,40},{40,32},{48,56},{56,48},{64,72... | collective-permute-start | bytes 9437192 | tf_op jit(solution)/shard_map/ppermute | solution.py:50
  21.8 13.6 %copy-start.4 = (bf16[6144]{0:T(1024)(128)(2,1)S(1)}, bf16[6144]{0:T(1024)(128)(2,1)}, u32[]{:S(2)}) copy-start(bf16[6144]{0:T(1024)(128)(2,1)} %param.22) | copy-start | bytes 36868
  21.9 36.1 %copy-start = (bf16[768,384]{1,0:T(8,128)(2,1)S(1)}, bf16[768,384]{1,0:T(8,128)(2,1)}, u32[]{:S(2)}) copy-start(bf16[768,384]{1,0:T(8,128)(2,1)} %own.1) | copy-start | bytes 1769476
  32.0 13.5 %all-to-all-start.1 = ((bf16[8,112,128]{2,1,0:T(8,128)(2,1)}), bf16[8,112,128]{2,1,0:T(8,128)(2,1)S(1)}, u32[]{:S(2)}, u32[]{:S(2)}) async-start(bf16[8,112,128]{2,1,0:T(8,128)(2,1)} %shard_map.138), calls=%async_computation.1 | async-start | bytes 458752 | tf_op jit(solution)/shard_map/all_to_all | solution.py:42
  45.8 49.5 %copy-start.1 = (bf16[1,6144]{1,0:T(2,128)(2,1)S(1)}, bf16[1,6144]{1,0:T(2,128)(2,1)}, u32[]{:S(2)}) copy-start(bf16[1,6144]{1,0:T(2,128)(2,1)} %get-tuple-element.23.gain) | copy-start | bytes 36868
  96.1 20.3 %copy-start.2 = (bf16[6144,4]{0,1:T(4,128)(2,1)S(1)}, bf16[6144,4]{0,1:T(4,128)(2,1)}, u32[]{:S(2)}) copy-start(bf16[6144,4]{0,1:T(4,128)(2,1)} %param.23) | copy-start | bytes 147460
  96.1 20.3 %copy-start.3 = (s32[256,2]{0,1:T(2,128)S(1)}, s32[256,2]{0,1:T(2,128)}, u32[]{:S(2)}) copy-start(s32[256,2]{0,1:T(2,128)} %param.24) | copy-start | bytes 6148
